TPU v7x, 128 devices: a whole 4x4x4 slice. The times are simulated.
128 devices in a mesh: rep: 8 (over x, core), graph: 16 (over y, z).
Axes of the slice: x: 4, y: 4, z: 4, core: 2. Of those that a mesh axis runs over, the one named last changes fastest.
Arguments:
- node_feats: bfloat16 [4096, 49, 128], P(('rep', 'graph')), may hold values from -6 to 6
- grad_out: bfloat16 [4096, 49, 128], P(('rep', 'graph')), may hold values from -6 to 6
- wigner: bfloat16 [235, 81920], P(None, ('rep', 'graph')), may hold values from -1.796875 to 1.796875
- weight_zero: bfloat16 [896, 896], replicated, may hold values from -0.1875 to 0.1875
- weight_one: bfloat16 [768, 2, 768], replicated, may hold values from -0.15625 to 0.15625
- weight_two: bfloat16 [640, 2, 640], replicated, may hold values from -0.15625 to 0.15625
- edge_source: int32 [81920], P(('rep', 'graph')), may hold values from 0 to 511
- edge_target: int32 [81920], P(('rep', 'graph')), may hold values from 0 to 31
- edge_count: int32 [128], P(('rep', 'graph')), may hold values from 320 to 640, as said below
Outputs:
- grad_feats: bfloat16 [4096, 49, 128], P(('rep', 'graph'))
- grad_zero: float32 [896, 896], P('graph')
- grad_one: float32 [768, 2, 768], P('graph')
- grad_two: float32 [640, 2, 640], P('graph')
Inputs may be any that keep to these rules, and one draw needn't show every extreme that they name: `edge_count`: at least half of a device's 640 slots are live, and some device has all 640 live.
All inputs are finite; a program needn't handle non-finite values.
Results may differ from a plain program's by a relative error of at most 0.015.
Values may be sent and summed in bfloat16 or wider, within the bound.
No kernel may reach another device: no remote copies, remote signals or barrier semaphores. Data moves between devices by JAX's collectives and lax.ppermute only.
A program may use at most 192 MiB of HBM per device.

v0:
```python
import jax
import jax.numpy as jnp
from jax import lax
from jax.sharding import PartitionSpec as P

LMAX = 6


def dot_wide(left, right):
    return jnp.dot(left, right, preferred_element_type=jnp.float32)


def over_edges(left, right):
    return lax.dot_general(
        left, right, (((0,), (0,)), ((), ())), preferred_element_type=jnp.float32
    )


def times_transpose(left, right):
    return lax.dot_general(
        left, right, (((1,), (1,)), ((), ())), preferred_element_type=jnp.float32
    )


def to_frame(turn_cols, features):
    frame_parts = {azimuth: [] for azimuth in range(-2, 3)}
    offset = 0
    for harmonic in range(LMAX + 1):
        kept_half = min(harmonic, 2)
        full_rows = 2 * harmonic + 1
        for row in range(2 * kept_half + 1):
            total = None
            for column in range(full_rows):
                factor = turn_cols[:, offset + row * full_rows + column][:, None]
                term = factor * features[:, harmonic * harmonic + column, :].astype(jnp.float32)
                total = term if total is None else total + term
            frame_parts[row - kept_half].append(total.astype(jnp.bfloat16))
        offset += (2 * kept_half + 1) * full_rows
    edge_total = features.shape[0]
    return {
        azimuth: jnp.stack(frame_parts[azimuth], axis=1).reshape(edge_total, -1)
        for azimuth in frame_parts
    }


def from_frame(turn_cols, frame_grads, channels):
    edge_total = turn_cols.shape[0]
    shaped = {
        azimuth: frame_grads[azimuth].reshape(edge_total, -1, channels) for azimuth in frame_grads
    }
    rows_out = []
    offset = 0
    for harmonic in range(LMAX + 1):
        kept_half = min(harmonic, 2)
        full_rows = 2 * harmonic + 1
        kept_slices = []
        for azimuth in range(-kept_half, kept_half + 1):
            kept_slices.append(shaped[azimuth][:, harmonic - abs(azimuth), :].astype(jnp.float32))
        for column in range(full_rows):
            total = None
            for row in range(2 * kept_half + 1):
                factor = turn_cols[:, offset + row * full_rows + column][:, None]
                term = factor * kept_slices[row]
                total = term if total is None else total + term
            rows_out.append(total.astype(jnp.bfloat16))
        offset += (2 * kept_half + 1) * full_rows
    return jnp.stack(rows_out, axis=1)


def edge_grads(sources, cotangent, wigner, weight_zero, weight_one, weight_two):
    channels = sources.shape[2]
    turn_cols = wigner.T.astype(jnp.float32)
    frame_x = to_frame(turn_cols, sources)
    frame_g = to_frame(turn_cols, cotangent)
    grad_zero = over_edges(frame_x[0], frame_g[0])
    frame_back = {0: times_transpose(frame_g[0], weight_zero).astype(jnp.bfloat16)}
    grad_pairs = []
    for azimuth, weights in ((1, weight_one), (2, weight_two)):
        real_part = weights[:, 0, :]
        imag_part = weights[:, 1, :]
        plus_x, minus_x = (frame_x[azimuth], frame_x[-azimuth])
        plus_g, minus_g = (frame_g[azimuth], frame_g[-azimuth])
        grad_real = over_edges(plus_x, plus_g) + over_edges(minus_x, minus_g)
        grad_imag = over_edges(plus_x, minus_g) - over_edges(minus_x, plus_g)
        grad_pairs.append(jnp.stack([grad_real, grad_imag], axis=1))
        frame_back[azimuth] = (
            times_transpose(plus_g, real_part) + times_transpose(minus_g, imag_part)
        ).astype(jnp.bfloat16)
        frame_back[-azimuth] = (
            times_transpose(minus_g, real_part) - times_transpose(plus_g, imag_part)
        ).astype(jnp.bfloat16)
    return (from_frame(turn_cols, frame_back, channels), grad_zero, grad_pairs[0], grad_pairs[1])


def per_device(
    node_feats,
    grad_out,
    wigner,
    weight_zero,
    weight_one,
    weight_two,
    edge_source,
    edge_target,
    edge_count,
):
    atom_local, coef_total, channels = node_feats.shape
    edge_total = edge_source.shape[0]
    flat_x = node_feats.reshape(atom_local, coef_total * channels)
    fragment = lax.all_gather(flat_x, "graph", axis=0, tiled=True)
    wanted = edge_source[:, None] == jnp.arange(fragment.shape[0], dtype=jnp.int32)[None, :]
    gathered = dot_wide(wanted.astype(jnp.bfloat16), fragment)
    sources = gathered.astype(jnp.bfloat16).reshape(edge_total, coef_total, channels)
    live_edges = jnp.arange(edge_total, dtype=jnp.int32) < edge_count[0]
    chosen = (
        edge_target[:, None] == jnp.arange(atom_local, dtype=jnp.int32)[None, :]
    ) & live_edges[:, None]
    cotangent = dot_wide(
        chosen.astype(jnp.bfloat16), grad_out.reshape(atom_local, coef_total * channels)
    )
    cotangent = cotangent.astype(jnp.bfloat16).reshape(edge_total, coef_total, channels)
    node_grad, grad_zero, grad_one, grad_two = edge_grads(
        sources, cotangent, wigner, weight_zero, weight_one, weight_two
    )
    flat_grad = node_grad.reshape(edge_total, coef_total * channels)
    owners = (
        jnp.arange(lax.axis_size("graph") * atom_local, dtype=jnp.int32)[:, None]
        == edge_source[None, :]
    )
    summed = lax.psum_scatter(
        dot_wide(owners.astype(jnp.bfloat16), flat_grad).astype(jnp.bfloat16),
        "graph",
        scatter_dimension=0,
        tiled=True,
    )
    grad_feats = summed.reshape(atom_local, coef_total, channels)
    graph_size = lax.axis_size("graph")
    scale = float(lax.axis_size("rep") * graph_size * edge_total) ** (-0.5)
    total_zero, total_one, total_two = lax.psum((grad_zero, grad_one, grad_two), ("rep", "graph"))
    position = lax.axis_index("graph")

    def own_rows(full_sum):
        row_share = full_sum.shape[0] // graph_size
        return lax.dynamic_slice_in_dim(full_sum, position * row_share, row_share, 0)

    shard_zero, shard_one, shard_two = (
        own_rows(total_zero),
        own_rows(total_one),
        own_rows(total_two),
    )
    return (grad_feats, shard_zero * scale, shard_one * scale, shard_two * scale)


def solution(mesh):
    in_specs = (
        P(("rep", "graph"), None, None),
        P(("rep", "graph"), None, None),
        P(None, ("rep", "graph")),
        P(),
        P(),
        P(),
        P(("rep", "graph")),
        P(("rep", "graph")),
        P(("rep", "graph")),
    )
    out_specs = (
        P(("rep", "graph"), None, None),
        P("graph", None),
        P("graph", None, None),
        P("graph", None, None),
    )
    return jax.shard_map(
        per_device, mesh=mesh, in_specs=in_specs, out_specs=out_specs, check_vma=False
    )
```

profile of v0, /device:TPU:1, one launch (start us, length us, event | category | flops | bytes accessed | tf_op | source)
XLA Modules:
  0.0 474.8 jit_solution(11021843247655952274)
XLA Ops:
  9.8 5.9 %convolution_convert_fusion.1 = bf16[640,6272]{1,0:T(8,128)(2,1)} fusion(s32[640]{0:T(1024)} %param.16, pred[640]{0:T(1024)(128)(4,1)S(1)} %iota_compare_fusion.5, bf16[32,49,128]{2,0,1:T(8,128)(2,1)} %param.10), kind=kOutput, calls=%fused_computation.1 | convolution fusion | flops 260956160 | bytes 8432768 | tf_op jit(solution)/shard_map/dot_general | solution.py:10
  15.7 11.8 %copy.27 = bf16[640,6272]{0,1:T(8,128)(2,1)} copy(bf16[640,6272]{1,0:T(8,128)(2,1)} %convolution_convert_fusion.1) | data formatting | bytes 16056320 | tf_op jit(solution)/shard_map/convert_element_type | solution.py:120
  31.4 2.3 constant_dynamic-update-slice_fusion.23
  37.2 2.3 constant_dynamic-update-slice_fusion.12
  42.2 2.5 convolution_convert_fusion.3
  44.8 2.6 copy.28
  56.4 2.2 constant_dynamic-update-slice_fusion.11
  60.3 2.2 constant_dynamic-update-slice_fusion.10
  66.1 2.5 constant_dynamic-update-slice_fusion.9
  72.6 2.6 constant_dynamic-update-slice_fusion.8
  77.2 2.7 fusion.715
  83.6 4.7 fusion.714
  89.6 2.2 fusion.3
  91.8 9.5 %convolution_convert_fusion = bf16[640,6272]{1,0:T(8,128)(2,1)} fusion(bf16[512,6272]{1,0:T(8,128)(2,1)} %all-gather.2.cloned.1.call-done, s32[640]{0:T(1024)S(1)} %copy-done.109), kind=kOutput, calls=%fused_computation | convolution fusion | flops 4114759680 | bytes 14453248 | tf_op jit(solution)/shard_map/dot_general | solution.py:10
  101.3 11.8 %copy.36 = bf16[640,6272]{0,1:T(8,128)(2,1)} copy(bf16[640,6272]{1,0:T(8,128)(2,1)} %convolution_convert_fusion) | data formatting | bytes 16056320 | tf_op jit(solution)/shard_map/convert_element_type | solution.py:112
  116.9 2.5 constant_dynamic-update-slice_fusion.89
  121.1 2.4 constant_dynamic-update-slice_fusion.16
  123.8 2.4 constant_dynamic-update-slice_fusion.15
  126.6 2.6 constant_dynamic-update-slice_fusion.14
  129.6 2.7 constant_dynamic-update-slice_fusion.13
  132.3 2.3 fusion.2
  134.6 2.5 fusion.718
  137.1 2.5 fusion.717
  153.1 2.2 subtract_convert_fusion
  156.8 2.3 copy.32
  159.1 3.5 subtract_bitcast_fusion
  163.9 2.5 constant_dynamic-update-slice_fusion.104
  203.5 3.2 fusion.716
  208.8 2.5 pad_maximum_fusion
  236.4 10.8 %convolution_convert_fusion.2 = bf16[512,6272]{1,0:T(8,128)(2,1)} fusion(bf16[640,6272]{0,1:T(8,128)(2,1)} %bitcast.409, s32[640]{0:T(1024)S(1)} %copy-done.110), kind=kOutput, calls=%fused_computation.2 | convolution fusion | flops 4113956864 | bytes 14453248 | tf_op jit(solution)/shard_map/dot_general | solution.py:10
  247.3 136.2 %all-reduce.3.cloned.1.call-done = (f32[896,896]{1,0:T(8,128)}, f32[768,2,768]{2,0,1:T(8,128)}, f32[640,2,640]{2,0,1:T(8,128)}) async-done(((f32[896,896]{1,0:T(8,128)}, f32[768,2,768]{2,0,1:T(8,128)}, f32[640,2,640]{2,0,1:T(8,128)}), (f32[896,896]{1,0:T(8,128)}, f32[768,2,768]{2,0,1:T(8,128)}, f32[640,2,640]{2,0,1:T(8,128)})) %all-reduce.3.cloned.1.call-update) | async-done | bytes 11206672 | tf_op jit(solution)/shard_map/psum | solution.py:138
  388.8 77.3 %reduce-scatter.2.cloned.1.call-done = bf16[32,6272]{1,0:T(8,128)(2,1)} async-done(((bf16[512,6272]{1,0:T(8,128)(2,1)}), bf16[32,6272]{1,0:T(8,128)(2,1)}) %reduce-scatter.2.cloned.1.call-update) | async-done | bytes 401424 | tf_op jit(solution)/shard_map/reduce_scatter | solution.py:129
  (359 shorter events, 130.5 us)
Async XLA Ops:
  7.2 35.1 %copy-start = (bf16[896,896]{1,0:T(8,128)(2,1)S(1)}, bf16[896,896]{1,0:T(8,128)(2,1)}, u32[]{:S(2)}) copy-start(bf16[896,896]{1,0:T(8,128)(2,1)} %param.12) | copy-start | bytes 4816900
  7.2 84.7 %all-gather.2.cloned.1.call-start = ((), (), s32[]{:S(2)}) async-start(), calls=%async_computation.2 | async-start | bytes 6823936 | tf_op jit(solution)/shard_map/all_gather | solution.py:109
  9.1 374.4 %all-reduce.3.cloned.1.call-start = ((), (), s32[]{:S(2)}) async-start(), calls=%async_computation.3 | async-start | bytes 22413312 | tf_op jit(solution)/shard_map/psum | solution.py:138
  29.0 92.0 %copy-start.68 = (f32[640]{0:T(1024)}, f32[640]{0:T(1024)S(1)}, u32[]{:S(2)}) copy-start(f32[640]{0:T(1024)S(1)} %get-tuple-element.127) | copy-start | bytes 7684
  29.0 92.0 %copy-start.80 = (f32[640]{0:T(1024)}, f32[640]{0:T(1024)S(1)}, u32[]{:S(2)}) copy-start(f32[640]{0:T(1024)S(1)} %get-tuple-element.128) | copy-start | bytes 7684
  29.0 92.0 %copy-start.82 = (f32[640]{0:T(1024)}, f32[640]{0:T(1024)S(1)}, u32[]{:S(2)}) copy-start(f32[640]{0:T(1024)S(1)} %get-tuple-element.129) | copy-start | bytes 7684
  29.0 92.1 %copy-start.86 = (f32[640]{0:T(1024)}, f32[640]{0:T(1024)S(1)}, u32[]{:S(2)}) copy-start(f32[640]{0:T(1024)S(1)} %get-tuple-element.130) | copy-start | bytes 7684
  29.0 92.1 %copy-start.90 = (f32[640]{0:T(1024)}, f32[640]{0:T(1024)S(1)}, u32[]{:S(2)}) copy-start(f32[640]{0:T(1024)S(1)} %get-tuple-element.131) | copy-start | bytes 7684
  31.4 31.2 %copy-start.102 = (f32[640]{0:T(1024)}, f32[640]{0:T(1024)S(1)}, u32[]{:S(2)}) copy-start(f32[640]{0:T(1024)S(1)} %get-tuple-element.89) | copy-start | bytes 7684
  31.4 31.2 %copy-start.104 = (f32[640]{0:T(1024)}, f32[640]{0:T(1024)S(1)}, u32[]{:S(2)}) copy-start(f32[640]{0:T(1024)S(1)} %get-tuple-element.88) | copy-start | bytes 7684
  56.4 18.7 %slice-start = ((s8[8028160]{0:T(1024)(128)(4,1)}), s8[4194304]{0:T(1024)(128)(4,1)S(1)}, s32[]{:S(2)}) async-start(s8[8028160]{0:T(1024)(128)(4,1)} %bitcast.115), calls=%async_computation.4 | async-start | bytes 8388608
  76.1 71.6 %copy-start.8 = (bf16[640,5,128]{0,2,1:T(8,128)(2,1)}, bf16[640,5,128]{0,2,1:T(8,128)(2,1)S(1)}, u32[]{:S(2)}) copy-start(bf16[640,5,128]{0,2,1:T(8,128)(2,1)S(1)} %constant_dynamic-update-slice_fusion.24) | copy-start | bytes 2457604
  166.5 14.7 %copy-start.63 = (f32[640]{0:T(1024)S(1)}, f32[640]{0:T(1024)}, u32[]{:S(2)}) copy-start(f32[640]{0:T(1024)} %copy-done.62) | copy-start | bytes 7684
  166.9 15.8 %copy-start.61 = (f32[640]{0:T(1024)S(1)}, f32[640]{0:T(1024)}, u32[]{:S(2)}) copy-start(f32[640]{0:T(1024)} %copy-done.60) | copy-start | bytes 7684
  166.9 15.8 %copy-start.83 = (f32[640]{0:T(1024)S(1)}, f32[640]{0:T(1024)}, u32[]{:S(2)}) copy-start(f32[640]{0:T(1024)} %copy-done.82) | copy-start | bytes 7684
  166.9 17.3 %copy-start.59 = (f32[640]{0:T(1024)S(1)}, f32[640]{0:T(1024)}, u32[]{:S(2)}) copy-start(f32[640]{0:T(1024)} %copy-done.58) | copy-start | bytes 7684
  166.9 17.3 %copy-start.81 = (f32[640]{0:T(1024)S(1)}, f32[640]{0:T(1024)}, u32[]{:S(2)}) copy-start(f32[640]{0:T(1024)} %copy-done.80) | copy-start | bytes 7684
  167.4 18.3 %copy-start.55 = (f32[640]{0:T(1024)S(1)}, f32[640]{0:T(1024)}, u32[]{:S(2)}) copy-start(f32[640]{0:T(1024)} %copy-done.54) | copy-start | bytes 7684
  167.4 18.3 %copy-start.95 = (f32[640]{0:T(1024)S(1)}, f32[640]{0:T(1024)}, u32[]{:S(2)}) copy-start(f32[640]{0:T(1024)} %copy-done.94) | copy-start | bytes 7684
  167.4 18.3 %copy-start.99 = (f32[640]{0:T(1024)S(1)}, f32[640]{0:T(1024)}, u32[]{:S(2)}) copy-start(f32[640]{0:T(1024)} %copy-done.98) | copy-start | bytes 7684
  168.9 17.1 %copy-start.69 = (f32[640]{0:T(1024)S(1)}, f32[640]{0:T(1024)}, u32[]{:S(2)}) copy-start(f32[640]{0:T(1024)} %copy-done.68) | copy-start | bytes 7684
  173.5 17.0 %copy-start.79 = (f32[640]{0:T(1024)S(1)}, f32[640]{0:T(1024)}, u32[]{:S(2)}) copy-start(f32[640]{0:T(1024)} %copy-done.78) | copy-start | bytes 7684
  175.0 16.4 %copy-start.77 = (f32[640]{0:T(1024)S(1)}, f32[640]{0:T(1024)}, u32[]{:S(2)}) copy-start(f32[640]{0:T(1024)} %copy-done.76) | copy-start | bytes 7684
  176.6 15.7 %copy-start.75 = (f32[640]{0:T(1024)S(1)}, f32[640]{0:T(1024)}, u32[]{:S(2)}) copy-start(f32[640]{0:T(1024)} %copy-done.74) | copy-start | bytes 7684
  178.1 15.0 %copy-start.51 = (f32[640]{0:T(1024)S(1)}, f32[640]{0:T(1024)}, u32[]{:S(2)}) copy-start(f32[640]{0:T(1024)} %copy-done.50) | copy-start | bytes 7684
  178.1 15.0 %copy-start.53 = (f32[640]{0:T(1024)S(1)}, f32[640]{0:T(1024)}, u32[]{:S(2)}) copy-start(f32[640]{0:T(1024)} %copy-done.52) | copy-start | bytes 7684
  178.1 15.0 %copy-start.65 = (f32[640]{0:T(1024)S(1)}, f32[640]{0:T(1024)}, u32[]{:S(2)}) copy-start(f32[640]{0:T(1024)} %copy-done.64) | copy-start | bytes 7684
  178.1 15.0 %copy-start.67 = (f32[640]{0:T(1024)S(1)}, f32[640]{0:T(1024)}, u32[]{:S(2)}) copy-start(f32[640]{0:T(1024)} %copy-done.66) | copy-start | bytes 7684
  178.1 15.0 %copy-start.71 = (f32[640]{0:T(1024)S(1)}, f32[640]{0:T(1024)}, u32[]{:S(2)}) copy-start(f32[640]{0:T(1024)} %copy-done.70) | copy-start | bytes 7684
  178.1 15.0 %copy-start.73 = (f32[640]{0:T(1024)S(1)}, f32[640]{0:T(1024)}, u32[]{:S(2)}) copy-start(f32[640]{0:T(1024)} %copy-done.72) | copy-start | bytes 7684
  213.3 252.7 %reduce-scatter.2.cloned.1.call-start = ((), (), s32[]{:S(2)}) async-start(), calls=%async_computation.1 | async-start | bytes 6823936 | tf_op jit(solution)/shard_map/reduce_scatter | solution.py:129
  236.4 231.5 %copy-start.1 = (bf16[896,896]{1,0:T(8,128)(2,1)S(1)}, bf16[896,896]{1,0:T(8,128)(2,1)}, u32[]{:S(2)}) copy-start(bf16[896,896]{1,0:T(8,128)(2,1)} %param.12) | copy-start | bytes 4816900
  (87 other events, 752.5 us)
Sparse Core Ops, SparseCore 0:
  10.8 65.1 all-gather.1
  213.4 169.9 all-reduce.2
  386.9 79.0 reduce-scatter.1
where the time goes:
time: 483 us; the launch traced here: 475 us
  waiting for transfers between devices  214 us (44%)
  other arithmetic  127 us (26%)
  matrix products  60.1 us (12%)
  local copies, waits for them, and re-layouts  58.2 us (12%)
  between operations  16.1 us (3%)
    psum x1, waiting for transfers between devices, per_device(): lax.psum((grad_zero, grad_one, grad_two), ('rep', 'graph'))  136 us
    unnamed x87, other arithmetic  110 us
    reduce_scatter x1, waiting for transfers between devices, per_device(): lax.psum_scatter(dot_wide(owners.astype(jnp.bfloat16), flat_grad).astype(...  77.3 us
    dot_general x3, matrix products, dot_wide(): return jnp.dot(left, right, preferred_element_type=jnp.float32)  26.2 us
    dot_general x9, matrix products, over_edges(): lax.dot_general(left, right, (((0,), (0,)), ((), ())), preferred_element_...  19.2 us
    dot_general x9, matrix products, times_transpose(): lax.dot_general(left, right, (((1,), (1,)), ((), ())), preferred_element_...  14.7 us
    slice x13, local copies, waits for them, and re-layouts, to_frame(): factor = turn_cols[:, offset + row * full_rows + column][:, None]  12.6 us
    convert_element_type x1, local copies, waits for them, and re-layouts, per_device(): cotangent.astype(jnp.bfloat16).reshape(edge_total, coef_total, channels)  11.8 us
  transfers between devices with their start and end apart: 3, of which 2 were waited for; matrix products, arithmetic and copies ran while one was open for 25% of the time, Pallas kernels for 0%

commit v1 on v0

v1 whole, which is shorter than its diff:
```python
import jax
import jax.numpy as jnp
from jax import lax
from jax.experimental import pallas as pl
from jax.experimental.pallas import tpu as pltpu
from jax.sharding import PartitionSpec as P

LMAX = 6
C = 128
PART_ROWS = 176
F32, BF16 = jnp.float32, jnp.bfloat16


def rot_offset(l):
    return sum((2 * min(i, 2) + 1) * (2 * i + 1) for i in range(l))


def rows_of(l):
    return 2 * min(l, 2) + 1


CH = 64


def turn(l, edges, rot_ref, in_ref, emit):
    kept, full, first = rows_of(l), 2 * l + 1, rot_offset(l)

    @pl.loop(0, edges // 128)
    def _(tile):
        e0 = pl.multiple_of(tile * 128, 128)
        for c0 in range(0, C, CH):
            acc = [None] * kept
            for n in range(full):
                x = in_ref[pl.ds(n * C + c0, CH), pl.ds(e0, 128)]
                for r in range(kept):
                    f = rot_ref[pl.ds(first + r * full + n, 1), pl.ds(e0, 128)]
                    t = f * x
                    acc[r] = t if acc[r] is None else acc[r] + t
            for r in range(kept):
                emit(r, c0, e0, acc[r])


def nt(a, b):
    return lax.dot_general(a, b, (((1,), (1,)), ((), ())), preferred_element_type=F32)


def tn(a, b):
    return lax.dot_general(a, b, (((0,), (0,)), ((), ())), preferred_element_type=F32)


def grad_kernel(count_ref, g_ref, wig_ref, w0_ref, w1_ref, w2_ref, src_ref, tgt_ref,
                g0_ref, g1_ref, g2_ref, part_ref,
                rot_ref, rows_ref, gv0_ref, gv1_ref, gv2_ref, gx_ref):
    edges = wig_ref.shape[1]
    atoms = g_ref.shape[1]
    parts = part_ref.shape[0]
    rot_ref[...] = wig_ref[...].astype(F32)
    slot = lax.broadcasted_iota(jnp.int32, (atoms, edges), 1)
    atom = lax.broadcasted_iota(jnp.int32, (atoms, edges), 0)
    chosen = jnp.where((tgt_ref[...] == atom) & (slot < count_ref[0]), 1.0, 0.0).astype(BF16)
    for l in range(LMAX + 1):
        kept, full = rows_of(l), 2 * l + 1
        half = kept // 2
        g = jnp.concatenate([g_ref[l * l + n] for n in range(full)], axis=1)
        rows_ref[: full * C, :] = tn(g, chosen)

        def emit(r, c0, e0, value, l=l, half=half):
            m = r - half
            v = value.astype(BF16)
            if m == 0:
                g0_ref[pl.ds(l * C + c0, CH), pl.ds(e0, 128)] = v
                return
            ref = g1_ref if abs(m) == 1 else g2_ref
            deep = ref.shape[0] // 2
            at = (l - abs(m)) * C + c0
            if m > 0:
                ref[pl.ds(at, CH), pl.ds(e0, 128)] = v
                ref[pl.ds(deep + at, CH), pl.ds(edges + e0, 128)] = -v
            else:
                ref[pl.ds(deep + at, CH), pl.ds(e0, 128)] = v
                ref[pl.ds(at, CH), pl.ds(edges + e0, 128)] = v

        turn(l, edges, rot_ref, rows_ref, emit)
    gv0_ref[...] = jnp.dot(w0_ref[...], g0_ref[...], preferred_element_type=F32).astype(BF16).astype(F32)
    for k in range(2):
        at = pl.ds(k * edges, edges)
        gv1_ref[:, at] = jnp.dot(w1_ref[...], g1_ref[:, at], preferred_element_type=F32).astype(BF16).astype(F32)
        gv2_ref[:, at] = jnp.dot(w2_ref[...], g2_ref[:, at], preferred_element_type=F32).astype(BF16).astype(F32)
    atom = lax.broadcasted_iota(jnp.int32, (parts * atoms, edges), 0)
    owners = jnp.where(src_ref[...] == atom, 1.0, 0.0).astype(BF16)
    for l in range(LMAX + 1):
        kept, full, first = rows_of(l), 2 * l + 1, rot_offset(l)
        half = kept // 2

        @pl.loop(0, edges // 128)
        def _(tile):
            e0 = pl.multiple_of(tile * 128, 128)
            for c0 in range(0, C, CH):
                s = []
                for r in range(kept):
                    m = r - half
                    ref = (gv0_ref, gv1_ref, gv2_ref)[abs(m)]
                    s.append(ref[pl.ds((l - abs(m)) * C + c0, CH), pl.ds((edges if m < 0 else 0) + e0, 128)])
                for n in range(full):
                    acc = None
                    for r in range(kept):
                        f = rot_ref[pl.ds(first + r * full + n, 1), pl.ds(e0, 128)]
                        t = f * s[r]
                        acc = t if acc is None else acc + t
                    gx_ref[pl.ds(n * C + c0, CH), pl.ds(e0, 128)] = acc.astype(BF16)

        out = nt(owners, gx_ref[: full * C, :]).astype(BF16)
        for n in range(full):
            part_ref[:, l * l + n] = out[:, n * C : (n + 1) * C].reshape(parts, atoms, C)


def weight_kernel(place_ref, x_ref, wig_ref, src_ref, g0_ref, g1_ref, g2_ref, mine0, mine1, mine2, mine3, their_ref,
                  rot_ref, rows_ref, v0_ref, v1_ref, v2_ref, slab_ref):
    mine_refs = (mine0, mine1, mine2, mine3)
    parts, _, atoms, _ = x_ref.shape
    edges = wig_ref.shape[1]
    rot_ref[...] = wig_ref[...].astype(F32)
    atom = lax.broadcasted_iota(jnp.int32, (parts * atoms, edges), 0)
    chosen = jnp.where(src_ref[...] == atom, 1.0, 0.0).astype(BF16)
    for l in range(LMAX + 1):
        kept, full = rows_of(l), 2 * l + 1
        half = kept // 2
        x = jnp.concatenate([x_ref[:, l * l + n].reshape(parts * atoms, C) for n in range(full)], axis=1)
        rows_ref[: full * C, :] = tn(x, chosen)

        def emit(r, c0, e0, value, l=l, half=half):
            m = r - half
            ref = (v0_ref, v1_ref, v2_ref)[abs(m)]
            ref[pl.ds((l - abs(m)) * C + c0, CH), pl.ds((edges if m < 0 else 0) + e0, 128)] = value.astype(BF16)

        turn(l, edges, rot_ref, rows_ref, emit)
    base = 0
    for v_ref, g_ref in ((v0_ref, g0_ref), (v1_ref, g1_ref), (v2_ref, g2_ref)):
        share = v_ref.shape[0] // parts
        width = g_ref.shape[0]
        for j in range(0, width, 256):
            wide = min(256, width - j)
            d = nt(v_ref[...], g_ref[j : j + wide, :])
            for k in range(0, wide, C):
                slab_ref[:, base : base + share, :] = d[:, k : k + C].reshape(parts, share, C)
                base += share
    slab_ref[:, base:, :] = jnp.zeros((parts, slab_ref.shape[1] - base, C), F32)
    part_rows = mine_refs[0].shape[1]
    x, core = place_ref[0], place_ref[1]
    for k in range(4):
        group = 2 * lax.rem(x + k, 4)
        at = pl.ds(pl.multiple_of((group + core) * part_rows, 8), part_rows)
        mine_refs[k][...] = slab_ref[:, at, :].astype(BF16)
        at = pl.ds(pl.multiple_of((group + 1 - core) * part_rows, 8), part_rows)
        their_ref[k] = slab_ref[:, at, :].astype(BF16)


VM = pl.BlockSpec(memory_space=pltpu.VMEM)
SM = pl.BlockSpec(memory_space=pltpu.SMEM)
S = jax.ShapeDtypeStruct


def grads(count, g, wig, w0, w1, w2, src, tgt, parts):
    coefs, atoms, _ = g.shape
    edges = wig.shape[1]
    rot = wig.shape[0]
    k0, k1, k2 = w0.shape[0], w1.shape[0], w2.shape[0]
    return pl.pallas_call(
        grad_kernel,
        out_shape=(S((k0, edges), BF16), S((2 * k1, 2 * edges), BF16), S((2 * k2, 2 * edges), BF16),
                   S((parts, coefs, atoms, C), BF16)),
        in_specs=[SM] + [VM] * 7,
        out_specs=[VM] * 4,
        scratch_shapes=[pltpu.VMEM((rot, edges), F32), pltpu.VMEM((13 * C, edges), F32),
                        pltpu.VMEM((k0, edges), F32), pltpu.VMEM((k1, 2 * edges), F32),
                        pltpu.VMEM((k2, 2 * edges), F32), pltpu.VMEM((13 * C, edges), BF16)],
        compiler_params=pltpu.CompilerParams(vmem_limit_bytes=60 << 20),
        name="grads",
    )(count, g, wig, w0, w1, w2, src, tgt)


def weights(place, x, wig, src, g0, g1, g2):
    edges = wig.shape[1]
    rot = wig.shape[0]
    parts = x.shape[0]
    k0, k1, k2 = g0.shape[0], g1.shape[0] // 2, g2.shape[0] // 2
    return pl.pallas_call(
        weight_kernel,
        out_shape=tuple(S((parts, PART_ROWS, C), BF16) for _ in range(4)) + (S((4, parts, PART_ROWS, C), BF16),),
        in_specs=[SM] + [VM] * 6,
        out_specs=[VM] * 5,
        scratch_shapes=[pltpu.VMEM((rot, edges), F32), pltpu.VMEM((13 * C, edges), F32),
                        pltpu.VMEM((k0, edges), BF16), pltpu.VMEM((k1, 2 * edges), BF16),
                        pltpu.VMEM((k2, 2 * edges), BF16), pltpu.VMEM((parts, 8 * PART_ROWS, C), F32)],
        compiler_params=pltpu.CompilerParams(vmem_limit_bytes=60 << 20),
        name="weights",
    )(place, x, wig, src, g0, g1, g2)


def graph_shift(dy, dz):
    return [(y * 4 + z, (y + dy) % 4 * 4 + (z + dz) % 4) for y in range(4) for z in range(4)]


def rep_shift(dx, dc):
    return [(x * 2 + c, (x + dx) % 4 * 2 + (c + dc) % 2) for x in range(4) for c in range(2)]


def send_rep(value, dx, dc):
    return lax.ppermute(value, "rep", rep_shift(dx, dc))


def add(*terms):
    total = terms[0].astype(F32)
    for t in terms[1:]:
        total = total + t.astype(F32)
    return total.astype(BF16)


def reduce_weights(mine, theirs):
    got = send_rep(theirs, 0, 1)
    r = [add(mine[k], got[k]) for k in range(4)]
    half = r[2].shape[0] // 2
    up = send_rep(r[2][:half], 1, 0)
    down = send_rep(r[2][half:], -1, 0)
    r1 = jnp.concatenate([add(r[1][:half], up), r[1][half:]])
    r3 = jnp.concatenate([r[3][:half], add(r[3][half:], down)])
    r0 = add(r[0], send_rep(r1, 1, 0), send_rep(r3, -1, 0))
    pieces = lax.all_to_all(r0, "graph", split_axis=0, concat_axis=0, tiled=True)
    total = pieces.astype(F32).sum(0)
    return lax.all_gather(total, "rep", axis=0, tiled=True)


def per_device(node_feats, grad_out, wigner, w0, w1, w2, edge_source, edge_target, edge_count):
    atoms, coefs, _ = node_feats.shape
    parts = lax.axis_size("graph")
    edges = edge_source.shape[0]
    x = lax.all_gather(node_feats.transpose(1, 0, 2), "graph", axis=0, tiled=False)
    src, tgt = edge_source[None], edge_target[None]
    g0, g1, g2, part = grads(
        edge_count, grad_out.transpose(1, 0, 2), wigner, w0, w1.reshape(w1.shape[0], -1), w2.reshape(w2.shape[0], -1), src, tgt, parts
    )
    grad_feats = lax.psum_scatter(part, "graph", scatter_dimension=0, tiled=False).transpose(1, 0, 2)
    rep = lax.axis_index("rep")
    place = jnp.stack([rep // 2, rep % 2])
    *mine, theirs = weights(place, x, wigner, src, g0, g1, g2)
    slab = reduce_weights(mine, theirs)
    scale = float(lax.axis_size("rep") * parts * edges) ** (-0.5)
    outs = []
    base = 0
    for w in (w0, w1, w2):
        share, tiles = w.shape[0] // parts, w[0].size // C
        rows = slab[base : base + share * tiles].reshape(tiles, share, C).transpose(1, 0, 2)
        outs.append(rows.reshape((share,) + w.shape[1:]) * scale)
        base += share * tiles
    return (grad_feats, *outs)


def solution(mesh):
    both = P(("rep", "graph"))
    edge_spec = P(("rep", "graph"))
    in_specs = (both, both, P(None, ("rep", "graph")), P(), P(), P(), edge_spec, edge_spec, edge_spec)
    out_specs = (both, P("graph"), P("graph"), P("graph"))
    return jax.shard_map(per_device, mesh=mesh, in_specs=in_specs, out_specs=out_specs, check_vma=False)
```

time: 483 us -> 191 us (0.40); the launches traced: 475 us -> 191 us
  waiting for transfers between devices: 214 us -> 53.7 us
  other arithmetic: 127 us -> 3.77 us
  Pallas kernels: 0 us -> 66.6 us
  matrix products: 60.1 us -> 0 us
  local copies, waits for them, and re-layouts: 58.2 us -> 8.96 us
  blocking collectives: 0 us -> 36 us
  starting transfers between devices: 0.12 us -> 6.86 us
    psum x1 -> x0, waiting for transfers between devices: 136 us -> none  [per_device(): lax.psum((grad_zero, grad_one, grad_two), ('rep', 'graph'))]
    unnamed x87 -> x0, other arithmetic: 110 us -> none
    reduce_scatter x1 -> x0, waiting for transfers between devices: 77.3 us -> none  [per_device(): lax.psum_scatter(dot_wide(owners.astype(jnp.bfloat16), flat_grad).astype(...]
    pallas_call x0 -> x2, Pallas kernels: none -> 66.6 us  [the longest x1 37 us: grads(): pl.pallas_call(grad_kernel, out_shape=(S((k0, edges), BF16), S((2 * k1, 2...]
    dot_general x21 -> x0, matrix products: 60.1 us -> none  [the longest x3 26.2 us: dot_wide(): return jnp.dot(left, right, preferred_element_type=jnp.float32)]
    ppermute x0 -> x5, waiting for transfers between devices: none -> 30 us  [send_rep(): return lax.ppermute(value, 'rep', rep_shift(dx, dc))]
    convert_element_type x5 -> x0, local copies, waits for them, and re-layouts: 29.9 us -> none  [the longest x1 11.8 us: per_device(): cotangent.astype(jnp.bfloat16).reshape(edge_total, coef_total, channels)]
    all_gather x1, waiting for transfers between devices: 0.01 us -> 22.9 us  [per_device(): lax.all_gather(node_feats.transpose(1, 0, 2), 'graph', axis=0, tiled=False)]
  transfers between devices with their start and end apart: 3 -> 7, of which waited for: 2 -> 5; matrix products, arithmetic and copies ran while one was open for 25% -> 7% of each run, Pallas kernels for 0% -> 35%
where the time goes in v1:
time: 191 us
  Pallas kernels  66.6 us (35%)
  waiting for transfers between devices  53.7 us (28%)
  blocking collectives  36 us (19%)
  between operations  14.8 us (8%)
  local copies, waits for them, and re-layouts  8.96 us (5%)
  starting transfers between devices  6.86 us (4%)
  other arithmetic  3.77 us (2%)
    pallas_call x1, Pallas kernels, grads(): pl.pallas_call(grad_kernel, out_shape=(S((k0, edges), BF16), S((2 * k1, 2...  37 us
    ppermute x5, waiting for transfers between devices, send_rep(): return lax.ppermute(value, 'rep', rep_shift(dx, dc))  30 us
    pallas_call x1, Pallas kernels, weights(): pl.pallas_call(weight_kernel, out_shape=tuple((S((parts, PART_ROWS, C), B...  29.6 us
    all_gather x1, waiting for transfers between devices, per_device(): lax.all_gather(node_feats.transpose(1, 0, 2), 'graph', axis=0, tiled=False)  22.9 us
    all_to_all x1, blocking collectives, reduce_weights(): lax.all_to_all(r0, 'graph', split_axis=0, concat_axis=0, tiled=True)  20.7 us
    all_gather x1, blocking collectives, reduce_weights(): return lax.all_gather(total, 'rep', axis=0, tiled=True)  15.3 us
    ppermute x5, starting transfers between devices, send_rep(): return lax.ppermute(value, 'rep', rep_shift(dx, dc))  6.78 us
    unnamed x10, local copies, waits for them, and re-layouts  5.17 us
  transfers between devices with their start and end apart: 7, of which 5 were waited for; matrix products, arithmetic and copies ran while one was open for 7% of the time, Pallas kernels for 35%

profile of v1, /device:TPU:1, one launch (start us, length us, event | category | flops | bytes accessed | tf_op | source)
XLA Modules:
  0.0 190.6 jit_solution(4857187877575116203)
XLA Ops:
  7.2 0.7 all-gather.3.cloned.1.call-update
  8.6 3.7 %copy.20 = bf16[96,8,2,768]{3,1,2,0:T(8,128)(2,1)} copy(bf16[96,8,2,768]{3,2,1,0:T(2,128)(2,1)} %bitcast.49) | data formatting | bytes 4718592
  12.3 1.5 copy.21
  13.8 0.6 broadcast_in_dim.6.src_ref
  14.3 0.6 broadcast_in_dim.7.tgt_ref
  14.9 37.0 %grads.1 = (bf16[896,640]{1,0:T(8,128)(2,1)}, bf16[1536,1280]{1,0:T(8,128)(2,1)}, bf16[1280,1280]{1,0:T(8,128)(2,1)}, bf16[16,49,32,128]{3,2,1,0:T(8,128)(2,1)}) custom-call(s32[1]{0:T(128)S(6)} %copy.24.count_ref, bf16[49,32,128]{2,1,0:T(8,128)(2,1)} %bitcast.55, bf16[235,640]{1,0:T(8,128)(2,1)} %wig_ref.3, bf16[896,896]{1,0:T(8,128)(2,1)} %w0_ref.1, ...), custom_call_target="tpu_custom_call" | custom-call | tf_op jit(solution)/shard_map/grads/pallas_call | solution.py:168
  52.0 0.6 pad_add_fusion.place_ref
  52.6 22.9 %all-gather.3.cloned.1.call-done = bf16[784,32,128]{2,1,0:T(8,128)(2,1)} async-done(((bf16[49,32,128]{2,1,0:T(8,128)(2,1)}), bf16[784,32,128]{2,1,0:T(8,128)(2,1)}) %all-gather.3.cloned.1.call-update) | async-done | bytes 6422544 | tf_op jit(solution)/shard_map/all_gather | solution.py:237
  75.5 29.6 %weights.1 = (bf16[16,176,128]{2,1,0:T(8,128)(2,1)}, bf16[16,176,128]{2,1,0:T(8,128)(2,1)}, bf16[16,176,128]{2,1,0:T(8,128)(2,1)}, bf16[16,176,128]{2,1,0:T(8,128)(2,1)}, bf16[4,16,176,128]{3,2,1,0:T(8,128)(2,1)}) custom-call(s32[2]{0:T(128)} %pad_add_fusion.place_ref, bf16[16,49,32,128]{3,2,1,0:T(8,128)(2,1)} %bitcast.48, bf16[235,640]{1,0:T(8,128)(2,1)} %wig_ref.3, ...), custom_call_target="tpu_custom_call" | custom-call | tf_op jit(solution)/shard_map/weights/pallas_call | solution.py:187
  105.0 0.7 collective-permute-start
  105.7 5.1 %collective-permute-done = bf16[4,16,176,128]{3,2,1,0:T(8,128)(2,1)S(1)} collective-permute-done((bf16[4,16,176,128]{3,2,1,0:T(8,128)(2,1)}, bf16[4,16,176,128]{3,2,1,0:T(8,128)(2,1)S(1)}, u32[]{:S(2)}, u32[]{:S(2)}) %collective-permute-start) | collective-permute-done | bytes 2883616 | tf_op jit(solution)/shard_map/ppermute | solution.py:209
  110.8 2.3 %fusion.2 = (bf16[16,176,128]{2,1,0:T(8,128)(2,1)S(1)}, bf16[16,176,128]{2,1,0:T(8,128)(2,1)S(1)}, bf16[16,176,128]{2,1,0:T(8,128)(2,1)S(1)}) fusion(bf16[16,176,128]{2,1,0:T(8,128)(2,1)} %get-tuple-element.19, bf16[4,16,176,128]{3,2,1,0:T(8,128)(2,1)S(1)} %collective-permute-done, bf16[16,176,128]{2,1,0:T(8,128)(2,1)} %get-tuple-element.21, ...), kind=kLoop, calls=%fused_computation.5 | loop fusion | flops 4325376 | bytes 6488064 | tf_op jit(solution)/shard_map/convert_element_type | solution.py:216
  113.2 2.5 %collective-permute-start.3 = (bf16[8,176,128]{2,1,0:T(8,128)(2,1)S(1)}, bf16[8,176,128]{2,1,0:T(8,128)(2,1)S(1)}, u32[]{:S(2)}, u32[]{:S(2)}) collective-permute-start(bf16[8,176,128]{2,1,0:T(8,128)(2,1)S(1)} %get-tuple-element.26), channel_id=1, source_target_pairs={{0,96},{16,112},{32,0},{48,16},{64,32},{80,48},{96,64},{112,80},{1... | collective-permute-start | bytes 1081352 | tf_op jit(solution)/shard_map/ppermute | solution.py:209
  115.7 0.1 collective-permute-start.1
  115.8 7.4 %collective-permute-done.3 = bf16[8,176,128]{2,1,0:T(8,128)(2,1)S(1)} collective-permute-done((bf16[8,176,128]{2,1,0:T(8,128)(2,1)S(1)}, bf16[8,176,128]{2,1,0:T(8,128)(2,1)S(1)}, u32[]{:S(2)}, u32[]{:S(2)}) %collective-permute-start.3) | collective-permute-done | bytes 360480 | tf_op jit(solution)/shard_map/ppermute | solution.py:209
  123.2 0.1 add_convert_fusion.1
  123.3 0.1 pad_maximum_fusion.1
  123.4 3.5 %collective-permute-start.4 = (bf16[16,176,128]{2,1,0:T(8,128)(2,1)S(1)}, bf16[16,176,128]{2,1,0:T(8,128)(2,1)S(1)}, u32[]{:S(2)}, u32[]{:S(2)}) collective-permute-start(bf16[16,176,128]{2,1,0:T(8,128)(2,1)S(1)} %pad_maximum_fusion.1), channel_id=1, source_target_pairs={{0,96},{16,112},{32,0},{48,16},{64,32},{80,48},{96,64},{112,80},{1... | collective-permute-start | bytes 2162696 | tf_op jit(solution)/shard_map/ppermute | solution.py:209
  126.9 0.1 add_convert_fusion.2
  127.0 0.1 pad_maximum_fusion
  127.1 0.1 collective-permute-start.2
  127.2 14.1 %collective-permute-done.4 = bf16[16,176,128]{2,1,0:T(8,128)(2,1)S(1)} collective-permute-done((bf16[16,176,128]{2,1,0:T(8,128)(2,1)S(1)}, bf16[16,176,128]{2,1,0:T(8,128)(2,1)S(1)}, u32[]{:S(2)}, u32[]{:S(2)}) %collective-permute-start.4) | collective-permute-done | bytes 720928 | tf_op jit(solution)/shard_map/ppermute | solution.py:209
  141.3 3.4 %collective-permute-done.2 = bf16[16,176,128]{2,1,0:T(8,128)(2,1)S(1)} collective-permute-done((bf16[16,176,128]{2,1,0:T(8,128)(2,1)S(1)}, bf16[16,176,128]{2,1,0:T(8,128)(2,1)S(1)}, u32[]{:S(2)}, u32[]{:S(2)}) %collective-permute-start.2) | collective-permute-done | bytes 720928 | tf_op jit(solution)/shard_map/ppermute | solution.py:209
  144.6 0.4 add_convert_fusion
  145.0 20.7 %all_to_all.5 = bf16[16,176,128]{2,1,0:T(8,128)(2,1)S(1)} all-to-all(bf16[16,176,128]{2,1,0:T(8,128)(2,1)S(1)} %add_convert_fusion), channel_id=1, replica_groups=mesh['rep'=8,'graph'=16] {'graph'}, dimensions={0} | all-to-all | bytes 1441792 | tf_op jit(solution)/shard_map/all_to_all | solution.py:228
  165.7 0.1 convert_reduce_fusion
  165.8 15.3 %all_gather.11 = f32[1408,128]{1,0:T(8,128)S(1)} all-gather(f32[176,128]{1,0:T(8,128)S(1)} %convert_reduce_fusion), channel_id=1, replica_groups=mesh['rep'=8,'graph'=16] {'rep'}, dimensions={0}, use_global_device_ids=true | all-gather | bytes 811008 | tf_op jit(solution)/shard_map/all_gather | solution.py:230
  181.1 0.7 copy.23
  181.9 0.1 copy.17
  182.0 0.9 mul.54
  182.9 0.1 copy.18
  182.9 0.8 mul.59
  (19 shorter events, 0.3 us)
Async XLA Ops:
  7.2 68.3 %all-gather.3.cloned.1.call-start = ((), (), s32[]{:S(2)}) async-start(), calls=%async_computation.2 | async-start | bytes 6823936 | tf_op jit(solution)/shard_map/all_gather | solution.py:237
  7.9 175.8 %reduce-scatter.4.cloned.1.call-start = ((), (), s32[]{:S(2)}) async-start(), calls=%async_computation.3 | async-start | bytes 6823936
  8.6 3.7 %copy-start = (bf16[640,2,640]{2,1,0:T(2,128)(2,1)S(1)}, bf16[640,2,640]{2,1,0:T(2,128)(2,1)}, u32[]{:S(2)}) copy-start(bf16[640,2,640]{2,1,0:T(2,128)(2,1)} %param.14) | copy-start | bytes 4915204
  12.3 1.5 copy-start.2
  12.3 2.1 %copy-start.3 = (s32[640]{0:T(1024)S(1)}, s32[640]{0:T(1024)}, u32[]{:S(2)}) copy-start(s32[640]{0:T(1024)} %param.16) | copy-start | bytes 7684
  105.0 5.8 %collective-permute-start = (bf16[4,16,176,128]{3,2,1,0:T(8,128)(2,1)}, bf16[4,16,176,128]{3,2,1,0:T(8,128)(2,1)S(1)}, u32[]{:S(2)}, u32[]{:S(2)}) collective-permute-start(bf16[4,16,176,128]{3,2,1,0:T(8,128)(2,1)} %get-tuple-element.18), channel_id=1, source_target_pairs={{0,16},{16,0},{32,48},{48,32},{64,80},{80,64},{96,112},{112,96},{1... | collective-permute-start | bytes 8650760 | tf_op jit(solution)/shard_map/ppermute | solution.py:209
  113.2 10.0 %collective-permute-start.3 = (bf16[8,176,128]{2,1,0:T(8,128)(2,1)S(1)}, bf16[8,176,128]{2,1,0:T(8,128)(2,1)S(1)}, u32[]{:S(2)}, u32[]{:S(2)}) collective-permute-start(bf16[8,176,128]{2,1,0:T(8,128)(2,1)S(1)} %get-tuple-element.26), channel_id=1, source_target_pairs={{0,96},{16,112},{32,0},{48,16},{64,32},{80,48},{96,64},{112,80},{1... | collective-permute-start | bytes 1081352 | tf_op jit(solution)/shard_map/ppermute | solution.py:209
  115.7 11.2 %collective-permute-start.1 = (bf16[8,176,128]{2,1,0:T(8,128)(2,1)S(1)}, bf16[8,176,128]{2,1,0:T(8,128)(2,1)S(1)}, u32[]{:S(2)}, u32[]{:S(2)}) collective-permute-start(bf16[8,176,128]{2,1,0:T(8,128)(2,1)S(1)} %get-tuple-element.25), channel_id=1, source_target_pairs={{0,32},{16,48},{32,64},{48,80},{64,96},{80,112},{96,0},{112,16},{1... | collective-permute-start | bytes 1081352 | tf_op jit(solution)/shard_map/ppermute | solution.py:209
  123.4 21.3 %copy-start.1 = (bf16[16,176,128]{2,1,0:T(8,128)(2,1)S(1)}, bf16[16,176,128]{2,1,0:T(8,128)(2,1)}, u32[]{:S(2)}) copy-start(bf16[16,176,128]{2,1,0:T(8,128)(2,1)} %get-tuple-element.17) | copy-start | bytes 2162692
  123.4 17.9 %collective-permute-start.4 = (bf16[16,176,128]{2,1,0:T(8,128)(2,1)S(1)}, bf16[16,176,128]{2,1,0:T(8,128)(2,1)S(1)}, u32[]{:S(2)}, u32[]{:S(2)}) collective-permute-start(bf16[16,176,128]{2,1,0:T(8,128)(2,1)S(1)} %pad_maximum_fusion.1), channel_id=1, source_target_pairs={{0,96},{16,112},{32,0},{48,16},{64,32},{80,48},{96,64},{112,80},{1... | collective-permute-start | bytes 2162696 | tf_op jit(solution)/shard_map/ppermute | solution.py:209
  127.1 17.6 %collective-permute-start.2 = (bf16[16,176,128]{2,1,0:T(8,128)(2,1)S(1)}, bf16[16,176,128]{2,1,0:T(8,128)(2,1)S(1)}, u32[]{:S(2)}, u32[]{:S(2)}) collective-permute-start(bf16[16,176,128]{2,1,0:T(8,128)(2,1)S(1)} %pad_maximum_fusion), channel_id=1, source_target_pairs={{0,32},{16,48},{32,64},{48,80},{64,96},{80,112},{96,0},{112,16},{1... | collective-permute-start | bytes 2162696 | tf_op jit(solution)/shard_map/ppermute | solution.py:209
Sparse Core Ops, SparseCore 0:
  10.2 65.2 all-gather.2
  79.5 84.9 reduce-scatter.3
